TPU v7x, 128 devices: a whole 4x4x4 slice. The times are simulated.
128 devices in a mesh: ctx: 8 (over y, x_hi), head: 16 (over z, x_lo, core).
Axes of the slice: x: 4 (x_hi: 2, x_lo: 2; x = x_hi * 2 + x_lo), y: 4, z: 4, core: 2. Of those that a mesh axis runs over, the one named last changes fastest.
Arguments:
- queries: bfloat16 [4096, 8192], P('ctx', 'head'), may hold values from -8 to 8
- prefix_kv: bfloat16 [16, 8192, 128], P('head', 'ctx'), may hold values from -8 to 8
- cand_kv: bfloat16 [16, 4096, 128], P('head', 'ctx'), may hold values from -8 to 8
- lengths: int32 [64], P('ctx'), may hold values from 1 to 64, 3072 in all
- out_weight: bfloat16 [8192, 8192], P(None, 'head'), may hold values from -0.0625 to 0.0625
Outputs:
- mixed: bfloat16 [4096, 8192], P('ctx', 'head')
Inputs may be any that keep to these rules, and one draw needn't show every extreme that they name: `lengths`: each candidate has at least one live token; some candidate has all 64 live.
All inputs are finite; a program needn't handle non-finite values. No bound on the sum of `lengths` on one device may be relied on, other than what follows from the above.
Results may differ from a plain program's by a relative error of at most 0.012.
Values may be sent and summed in bfloat16 or wider, within the bound.
A program may use at most 192 MiB of HBM per device.

v0:
```python
import jax
import jax.numpy as jnp
from jax import lax
from jax.sharding import PartitionSpec as P

NEG_FILL = -1e30


def swapped(block, axis, apart):
    count = lax.axis_size(axis)
    route = []
    for low in range(count):
        high = low | 1 << apart
        if high != low and high < count:
            route += [(low, high), (high, low)]
    return lax.ppermute(block, axis, route)


def absorb(carried, query_block, key_block, value_block, score_scale):
    numerator, row_max, row_total = carried
    scores = (
        jnp.einsum("rhd,pd->hrp", query_block, key_block, preferred_element_type=jnp.float32)
        * score_scale
    )
    new_max = jnp.maximum(row_max, jnp.max(scores, axis=2))
    shrink = jnp.exp(row_max - new_max)
    probs = jnp.exp(scores - new_max[..., None])
    row_total = row_total * shrink + jnp.sum(probs, axis=2)
    numerator = numerator * shrink[..., None] + jnp.einsum(
        "hrp,pd->hrd", probs.astype(jnp.bfloat16), value_block, preferred_element_type=jnp.float32
    )
    return (numerator, new_max, row_total)


def body(queries, prefix_kv, cand_kv, lengths, out_weight):
    head_size = prefix_kv.shape[2]
    score_scale = head_size ** (-0.5)
    cand_rows = cand_kv.shape[1]
    pre_rows = prefix_kv.shape[1]
    cand_count = lengths.shape[0]
    step_tokens = cand_rows // cand_count
    local_heads = queries.shape[1] // head_size
    query_heads = queries.reshape(cand_rows, local_heads, head_size)
    stacked = jnp.concatenate([prefix_kv, cand_kv], axis=1)
    partner = swapped(stacked, "head", 0)
    holds_keys = lax.axis_index("head") % 2 == 0
    key_rows = jnp.where(holds_keys, stacked[0], partner[0])
    value_rows = jnp.where(holds_keys, partner[0], stacked[0])
    pre_keys, suffix_keys = (key_rows[:pre_rows], key_rows[pre_rows:])
    pre_vals, suffix_vals = (value_rows[:pre_rows], value_rows[pre_rows:])
    offsets = jnp.arange(step_tokens, dtype=jnp.int32)
    visible = (offsets[None, :] <= offsets[:, None])[None] & (
        offsets[None, None, :] < lengths[:, None, None]
    )
    suffix_scores = (
        jnp.einsum(
            "cthd,csd->hcts",
            query_heads.reshape(cand_count, step_tokens, local_heads, head_size),
            suffix_keys.reshape(cand_count, step_tokens, head_size),
            preferred_element_type=jnp.float32,
        )
        * score_scale
    )
    suffix_scores = jnp.where(visible[None], suffix_scores, NEG_FILL)
    suffix_max = jnp.max(suffix_scores, axis=3)
    suffix_probs = jnp.where(visible[None], jnp.exp(suffix_scores - suffix_max[..., None]), 0.0)
    suffix_total = jnp.sum(suffix_probs, axis=3).reshape(local_heads, cand_rows)
    suffix_numer = jnp.einsum(
        "hcts,csd->hctd",
        suffix_probs.astype(jnp.bfloat16),
        suffix_vals.reshape(cand_count, step_tokens, head_size),
        preferred_element_type=jnp.float32,
    ).reshape(local_heads, cand_rows, head_size)
    suffix_max = suffix_max.reshape(local_heads, cand_rows)
    numerator, row_max, row_total = absorb(
        (suffix_numer, suffix_max, suffix_total),
        query_heads,
        lax.all_gather(pre_keys, "ctx", axis=0, tiled=True),
        lax.all_gather(pre_vals, "ctx", axis=0, tiled=True),
        score_scale,
    )
    attended = (numerator / row_total[..., None]).astype(jnp.bfloat16)
    attended = attended.transpose(1, 0, 2).reshape(cand_rows, local_heads * head_size)
    projected = jnp.dot(
        lax.all_gather(attended, "head", axis=1, tiled=True),
        out_weight,
        preferred_element_type=jnp.float32,
    )
    return projected.astype(jnp.bfloat16)


def solution(mesh):
    placed = (
        P("ctx", "head"),
        P("head", "ctx", None),
        P("head", "ctx", None),
        P("ctx"),
        P(None, "head"),
    )
    return jax.shard_map(
        body, mesh=mesh, in_specs=placed, out_specs=P("ctx", "head"), check_vma=False
    )
```

profile of v0, /device:TPU:1, one launch (start us, length us, event | category | flops | bytes accessed | tf_op | source)
XLA Modules:
  0.0 216.9 jit_solution(18037234477038592657)
XLA Ops:
  6.5 0.0 all-gather.8.cloned.1.call-start
  6.5 1.0 constant_dynamic-update-slice_fusion.1
  7.5 0.9 constant_dynamic-update-slice_fusion
  8.4 1.5 collective-permute-start
  9.9 1.3 collective-permute-done
  11.3 0.1 broadcast_select_fusion
  11.3 0.7 slice.28
  12.1 0.0 all-gather.8.cloned.1.call-update
  12.1 0.0 all-gather.10.cloned.1.call-start
  12.1 1.2 reshape_reshape.3
  13.3 0.7 iota_compare_fusion.1
  14.0 0.1 broadcast_and_fusion
  14.2 0.7 slice.29
  14.9 0.7 fusion.36
  15.6 0.1 reshape.101
  15.7 0.3 fusion.25
  16.0 0.1 reshape.103
  16.1 0.4 convolution_bitcast_fusion
  16.4 0.1 copy.29
  16.6 0.3 copy.32
  16.9 0.0 all-gather.10.cloned.1.call-update
  16.9 0.2 all-gather.6.cloned.1.call-start
  17.1 50.7 %all-gather.8.cloned.1.call-done = bf16[1,8192,128]{2,1,0:T(8,128)(2,1)} async-done(((bf16[1,1024,128]{2,1,0:T(8,128)(2,1)}), bf16[1,8192,128]{2,1,0:T(8,128)(2,1)}) %all-gather.8.cloned.1.call-update) | async-done | bytes 2097168 | tf_op jit(solution)/shard_map/all_gather | solution.py:78
  67.9 25.8 %bitcast_reduce_fusion = (f32[4,512]{1,0:T(4,128)S(1)}, f32[8192,512,4]{1,0,2:T(8,128)}) fusion(bf16[1,8192,128]{2,1,0:T(8,128)(2,1)} %all-gather.8.cloned.1.call-done, bf16[512,512]{1,0:T(8,128)(2,1)} %param.5), kind=kOutput, calls=%fused_computation.1 | convolution fusion | flops 4328519680 | bytes 69738496 | tf_op jit(solution)/shard_map/rhd,pd->hrp/dot_general | solution.py:22
  93.7 22.1 %fusion.1 = f32[4,512]{1,0:T(4,128)S(1)} fusion(f32[8192,512,4]{1,0,2:T(8,128)} %get-tuple-element.12, f32[4,512]{1,0:T(4,128)S(1)} %max.13), kind=kLoop, calls=%fused_computation.3 | loop fusion | flops 50329600 | bytes 67125248 | tf_op jit(solution)/shard_map/reduce_sum | solution.py:28
  115.8 6.2 %all-gather.10.cloned.1.call-done = bf16[1,8192,128]{2,1,0:T(8,128)(2,1)} async-done(((bf16[1,1024,128]{2,1,0:T(8,128)(2,1)}), bf16[1,8192,128]{2,1,0:T(8,128)(2,1)}) %all-gather.10.cloned.1.call-update) | async-done | bytes 2097168 | tf_op jit(solution)/shard_map/all_gather | solution.py:79
  122.0 26.2 %fusion.20 = bf16[4,512,128]{1,2,0:T(8,128)(2,1)} fusion(bf16[1,8192,128]{2,1,0:T(8,128)(2,1)} %all-gather.10.cloned.1.call-done, f32[8192,512,4]{1,0,2:T(8,128)} %get-tuple-element.12, f32[4,512]{1,0:T(4,128)S(1)} %max.13, f32[4,512,128]{1,2,0:T(8,128)S(1)} %copy.32, f32[4,512]{1,0:T(4,128)S(1)} %get-tuple-element.5, f32[4,512]{1,0:T(4,128)S(1)} %get-tuple-element.6), kind=kOutput, calls=%fused_computation.16 | convolution fusion | flops 4346347520 | bytes 70803456 | tf_op jit(solution)/shard_map/hrp,pd->hrd/dot_general | solution.py:29
  148.2 0.0 all-gather.6.cloned.1.call-update
  148.3 51.0 %all-gather.6.cloned.1.call-done = bf16[512,8192]{0,1:T(8,128)(2,1)} async-done(((bf16[512,512]{0,1:T(8,128)(2,1)}), bf16[512,8192]{0,1:T(8,128)(2,1)}) %all-gather.6.cloned.1.call-update) | async-done | bytes 8388624 | tf_op jit(solution)/shard_map/all_gather | solution.py:85
  199.3 11.1 %convolution_convert_fusion = bf16[512,512]{1,0:T(8,128)(2,1)} fusion(bf16[512,8192]{0,1:T(8,128)(2,1)} %all-gather.6.cloned.1.call-done, bf16[8192,512]{1,0:T(8,128)(2,1)} %param.9), kind=kOutput, calls=%fused_computation.13 | convolution fusion | flops 4295229440 | bytes 17301504 | tf_op jit(solution)/shard_map/dot_general | solution.py:84
  (7 shorter events, 0.1 us)
Async XLA Ops:
  6.5 61.3 %all-gather.8.cloned.1.call-start = ((), (), s32[]{:S(2)}) async-start(), calls=%async_computation.1 | async-start | bytes 2359296 | tf_op jit(solution)/shard_map/all_gather | solution.py:78
  8.4 2.9 %collective-permute-start = (bf16[1,1536,128]{2,1,0:T(8,128)(2,1)S(1)}, bf16[1,1536,128]{2,1,0:T(8,128)(2,1)S(1)}, u32[]{:S(2)}, u32[]{:S(2)}) collective-permute-start(bf16[1,1536,128]{2,1,0:T(8,128)(2,1)S(1)} %constant_dynamic-update-slice_fusion), channel_id=1, source_target_pairs={{0,1},{1,0},{2,3},{3,2},{4,5},{5,4},{6,7},{7,6},{8,9},{9,8},{10,11... | collective-permute-start | bytes 1179656 | tf_op jit(solution)/shard_map/ppermute | solution.py:16
  12.1 109.9 %all-gather.10.cloned.1.call-start = ((), (), s32[]{:S(2)}) async-start(), calls=%async_computation.2 | async-start | bytes 2359296 | tf_op jit(solution)/shard_map/all_gather | solution.py:79
  16.9 182.4 %all-gather.6.cloned.1.call-start = ((), (), s32[]{:S(2)}) async-start(), calls=%async_computation | async-start | bytes 8912896 | tf_op jit(solution)/shard_map/all_gather | solution.py:85
Sparse Core Ops, SparseCore 0:
  12.2 55.6 all-gather.7
  70.2 51.7 all-gather.9
  148.4 50.8 all-gather.5
where the time goes:
time: 217 us
  waiting for transfers between devices  109 us (50%)
  matrix products  64.1 us (30%)
  other arithmetic  23.3 us (11%)
  between operations  13.2 us (6%)
  local copies, waits for them, and re-layouts  5.11 us (2%)
    all_gather x1, waiting for transfers between devices, body(): lax.all_gather(attended, 'head', axis=1, tiled=True)  51 us
    all_gather x1, waiting for transfers between devices, body(): lax.all_gather(pre_keys, 'ctx', axis=0, tiled=True)  50.7 us
    dot_general x1, matrix products, absorb(): jnp.einsum('hrp,pd->hrd', probs.astype(jnp.bfloat16), value_block, prefer...  26.2 us
    dot_general x1, matrix products, absorb(): jnp.einsum('rhd,pd->hrp', query_block, key_block, preferred_element_type=...  25.8 us
    reduce_sum x1, other arithmetic, absorb(): row_total = row_total * shrink + jnp.sum(probs, axis=2)  22.1 us
    dot_general x1, matrix products, body(): jnp.dot(lax.all_gather(attended, 'head', axis=1, tiled=True), out_weight,...  11.1 us
    all_gather x1, waiting for transfers between devices, body(): lax.all_gather(pre_vals, 'ctx', axis=0, tiled=True)  6.24 us
  transfers between devices with their start and end apart: 4, of which 4 were waited for; matrix products, arithmetic and copies ran while one was open for 24% of the time, Pallas kernels for 0%

commit v1 on v0

v1 whole, which is shorter than its diff:
```python
import functools
import math

import jax
import jax.numpy as jnp
from jax import lax
from jax.experimental import pallas as pl
from jax.experimental.pallas import tpu as pltpu
from jax.sharding import PartitionSpec as P

MESH = pl.DeviceIdType.MESH
BF = jnp.bfloat16
F32 = jnp.float32
NEG_FILL = -1e30
NT = (((1,), (1,)), ((), ()))

FORWARD, BACK, ACROSS, OVER = 0, 1, 2, 3
KINDS = 15


def attend_kernel(
    lengths_ref, q_hbm, pre_hbm, cand_hbm, w_hbm, out_ref,
    kv, cand, q_raw, q_two, weights, acc, row_max, att, total,
    local_sem, cand_sem, s1, r1, b1, s2, r2, b2,
):
    ctx, head = lax.axis_index("ctx"), lax.axis_index("head")
    y, x_hi = ctx // 2, ctx % 2
    z, x_lo, core = head // 4, (head // 2) % 2, head % 2

    def ring1(d):
        return (lax.rem(y + d, 4) * 2 + x_hi, head)

    def ring2(d):
        return (ctx, lax.rem(z + d, 4) * 4 + x_lo * 2 + core)

    over1 = (y * 2 + 1 - x_hi, head)
    over2 = (ctx, z * 4 + (1 - x_lo) * 2 + core)
    sibling = (ctx, z * 4 + x_lo * 2 + 1 - core)
    near1 = {FORWARD: ring1(1), BACK: ring1(3), ACROSS: ring1(2), OVER: over1}
    near2 = {FORWARD: ring2(1), BACK: ring2(3), ACROSS: ring2(2), OVER: over2}

    barrier = pltpu.get_barrier_semaphore()
    others = [*near1.values(), *near2.values(), sibling]
    for other in others:
        pl.semaphore_signal(barrier, inc=1, device_id=other, device_id_type=MESH)

    local = [
        pltpu.make_async_copy(pre_hbm.at[0], kv.at[core, 0], local_sem.at[0]),
        pltpu.make_async_copy(cand_hbm.at[0], cand.at[core], local_sem.at[1]),
        pltpu.make_async_copy(q_hbm, q_raw, local_sem.at[2]),
        pltpu.make_async_copy(w_hbm, weights, local_sem.at[3]),
    ]
    for copy in local[:3]:
        copy.start()

    def remote(src, dst, send, recv, device):
        return pltpu.make_async_remote_copy(
            src_ref=src, dst_ref=dst, send_sem=send, recv_sem=recv, device_id=device, device_id_type=MESH
        )

    rows1 = kv.shape[2] // CHUNKS1

    def piece1(slot, c):
        return kv.at[core, slot, pl.ds(c * rows1, rows1)]

    def piece2(slot, c):
        return att.at[slot, core, c]

    sent = []

    def send(phase, src_slot, dst_slot, c, kind, device):
        piece, ss, rr = (piece1, s1, r1) if phase == 1 else (piece2, s2, r2)
        src = piece(src_slot, c)
        if phase == 1 and src_slot == 0:
            src = pre_hbm.at[0, pl.ds(c * rows1, rows1)]
        copy = remote(src, piece(dst_slot, c), ss.at[kind, c], rr.at[dst_slot, c], device)
        copy.start()
        sent.append(copy)

    def share(phase, slot, c):
        piece, ss, bb = (piece1, s1, b1) if phase == 1 else (piece2, s2, b2)
        src = piece(slot, c)
        if phase == 1 and slot == 0:
            src = pre_hbm.at[0, pl.ds(c * rows1, rows1)]
        copy = remote(src, piece(slot, c), ss.at[7 + slot, c], bb.at[slot, c], sibling)
        copy.start()
        sent.append(copy)

    def arrived(phase, slot, c):
        piece, rr = (piece1, r1) if phase == 1 else (piece2, r2)
        ref = piece(slot, c)
        remote(ref, ref, rr.at[slot, c], rr.at[slot, c], sibling).wait_recv()

    def shared(phase, slot, c):
        if phase == 1:
            ref, bb = kv.at[1 - core, slot, pl.ds(c * rows1, rows1)], b1
        else:
            ref, bb = att.at[slot, 1 - core, c], b2
        remote(ref, ref, bb.at[slot, c], bb.at[slot, c], sibling).wait_recv()

    def near(phase):
        return near1 if phase == 1 else near2

    def own_near(phase, c):
        n = near(phase)
        send(phase, 0, 1, c, 3, n[OVER])
        send(phase, 0, 3, c, 0, n[FORWARD])
        send(phase, 0, 2, c, 1, n[BACK])

    def own_far(phase, c):
        send(phase, 0, 4, c, 2, near(phase)[ACROSS])

    def on_partner(phase, c):
        arrived(phase, 1, c)
        n = near(phase)
        send(phase, 1, 6, c, 4, n[FORWARD])
        send(phase, 1, 5, c, 5, n[BACK])
        share(phase, 1, c)

    def on_far(phase, c):
        arrived(phase, 4, c)
        send(phase, 4, 7, c, 6, near(phase)[OVER])
        share(phase, 4, c)

    def on_plain(phase, slot, c):
        arrived(phase, slot, c)
        share(phase, slot, c)

    pl.semaphore_wait(barrier, len(others))

    cand_copy = remote(cand_hbm.at[0], cand.at[core], cand_sem.at[0], cand_sem.at[1], sibling)
    cand_copy.start()
    for c in range(CHUNKS1):
        own_near(1, c)
    for c in range(CHUNKS1):
        share(1, 0, c)
    for c in range(CHUNKS1):
        own_far(1, c)
    local[3].start()

    heads = q_two.shape[0]
    hd = kv.shape[3]
    factor = hd ** (-0.5) * math.log2(math.e)
    local[2].wait()
    for h in range(heads):
        scaled = q_raw[:, h * hd : (h + 1) * hd].astype(F32) * factor
        high = scaled.astype(BF)
        q_two[h, :, :hd] = high
        q_two[h, :, hd:] = (scaled - high.astype(F32)).astype(BF)

    tokens = q_two.shape[1]
    half = tokens // 2
    pairs = [(h, r) for h in range(heads) for r in (0, half)]

    def twice(k):
        return jnp.concatenate([k, k], axis=1)

    def with_ones(v):
        return jnp.concatenate([v, jnp.ones_like(v)], axis=1)

    def scores(h, r, keys):
        return lax.dot_general(q_two[h, r : r + half], twice(keys), NT, preferred_element_type=F32)

    def ahead(units, first, second):
        held = first(*units[0])
        for i, unit in enumerate(units):
            following = first(*units[i + 1]) if i + 1 < len(units) else None
            second(held, *unit)
            held = following

    local[1].wait()
    remote(cand.at[1 - core], cand.at[1 - core], cand_sem.at[0], cand_sem.at[1], sibling).wait_recv()
    slots = tokens // lengths_ref.shape[0]
    per = half // slots
    row = lax.broadcasted_iota(jnp.int32, (half, half), 0)
    col = lax.broadcasted_iota(jnp.int32, (half, half), 1)
    row_cand, col_cand = row // slots, col // slots
    causal = (row_cand == col_cand) & (col <= row)
    masks = []
    for part in range(2):
        limit = jnp.zeros((half, half), jnp.int32)
        for j in range(per):
            limit = jnp.where(col_cand == j, lengths_ref[part * per + j] + j * slots, limit)
        masks.append(causal & (col < limit))

    def suffix_scores(h, r):
        return jnp.where(masks[r // half], scores(h, r, cand[0, r : r + half]), NEG_FILL)

    def suffix_rest(s, h, r):
        top = jnp.max(s, axis=1, keepdims=True)
        probs = jnp.exp2(s - top).astype(BF)
        acc[h, r : r + half] = jnp.dot(probs, with_ones(cand[1, r : r + half]), preferred_element_type=F32)
        row_max[h, r : r + half] = jnp.broadcast_to(top, (half, hd))

    ahead(pairs, suffix_scores, suffix_rest)

    def absorb(s, h, r, values, last):
        old = row_max[h, r : r + half]
        new = jnp.maximum(old, jnp.max(s, axis=1, keepdims=True))
        shrink = jnp.exp2(old - new)
        probs = jnp.exp2(s - new[:, :1]).astype(BF)
        added = jnp.dot(probs, with_ones(values), preferred_element_type=F32)
        result = acc[h, r : r + half] * jnp.concatenate([shrink, shrink], axis=1) + added
        if last:
            att[0, core, h, r : r + half] = (result[:, :hd] / result[:, hd:]).astype(BF)
        else:
            acc[h, r : r + half] = result
            row_max[h, r : r + half] = new

    def block(slot, chosen):
        ahead(
            chosen,
            lambda h, r: scores(h, r, kv[0, slot]),
            lambda s, h, r: absorb(s, h, r, kv[1, slot], False),
        )

    def both(slot):
        return kv[0, slot], kv[1, slot]

    every1 = range(CHUNKS1)
    local[0].wait()
    for c in every1:
        shared(1, 0, c)
    block(0, pairs)
    for c in every1:
        on_partner(1, c)
    for slot in (2, 3):
        for c in every1:
            on_plain(1, slot, c)
    for c in every1:
        shared(1, 1, c)
    block(1, pairs)
    for c in every1:
        on_far(1, c)
    for c in every1:
        shared(1, 2, c)
    block(2, pairs)
    for slot in (5, 6):
        for c in every1:
            on_plain(1, slot, c)
    for c in every1:
        shared(1, 3, c)
    block(3, pairs)
    for c in every1:
        on_plain(1, 7, c)
    for slot in (4, 5, 6, 7):
        for c in every1:
            shared(1, slot, c)

    def finish(h):
        units = [(h, r, j) for j in (0, 1) for r in (0, half)]

        def first(h, r, j):
            k = jnp.concatenate([kv[0, 4 + 2 * j], kv[0, 5 + 2 * j]], axis=0)
            return scores(h, r, k)

        def second(s, h, r, j):
            v = jnp.concatenate([kv[1, 4 + 2 * j], kv[1, 5 + 2 * j]], axis=0)
            absorb(s, h, r, v, j == 1)

        ahead(units, first, second)

    wide = total.shape[1]

    def project(slot, pair, first=False):
        dz = (0, 0, 1, 3, 2, 1, 3, 2)[slot]
        dx = (0, 1, 0, 0, 0, 1, 1, 1)[slot]
        group = lax.rem(z + dz, 4) * 2 + lax.rem(x_lo + dx, 2)
        base = group * (2 * heads * hd) + pair * 2 * hd
        pieces, sides = [], []
        for k in (0, 1):
            pieces += [att[slot, k, 2 * pair], att[slot, k, 2 * pair + 1]]
            start = pl.multiple_of(base + k * heads * hd, 2 * hd)
            sides.append(weights[pl.ds(start, 2 * hd), :])
        product = jnp.dot(
            jnp.concatenate(pieces, axis=1), jnp.concatenate(sides, axis=0), preferred_element_type=F32
        )
        total[...] = product if first else total[...] + product

    def launch(c):
        own_near(2, c)
        share(2, 0, c)
        own_far(2, c)

    finish(0)
    launch(0)
    finish(1)
    launch(1)
    finish(2)
    launch(2)
    on_partner(2, 0)
    finish(3)
    launch(3)

    def near_slots(c):
        on_plain(2, 2, c)
        on_plain(2, 3, c)

    def late_slots(c):
        on_plain(2, 5, c)
        on_plain(2, 6, c)

    def ready(slot, pair):
        shared(2, slot, 2 * pair)
        shared(2, slot, 2 * pair + 1)

    near_slots(0)
    on_partner(2, 1)
    on_far(2, 0)
    local[3].wait()
    ready(0, 0)
    project(0, 0, True)
    near_slots(1)
    late_slots(0)
    on_partner(2, 2)
    on_far(2, 1)
    on_plain(2, 7, 0)
    ready(1, 0)
    project(1, 0)
    near_slots(2)
    on_partner(2, 3)
    late_slots(1)
    ready(2, 0)
    project(2, 0)
    ready(3, 0)
    project(3, 0)
    on_far(2, 2)
    ready(4, 0)
    project(4, 0)
    on_plain(2, 7, 1)
    near_slots(3)
    ready(5, 0)
    project(5, 0)
    late_slots(2)
    ready(6, 0)
    project(6, 0)
    on_far(2, 3)
    ready(7, 0)
    project(7, 0)
    on_plain(2, 7, 2)
    for slot in (0, 1, 2, 3):
        ready(slot, 1)
        project(slot, 1)
    late_slots(3)
    ready(4, 1)
    project(4, 1)
    on_plain(2, 7, 3)
    for slot in (5, 6, 7):
        ready(slot, 1)
        project(slot, 1)
    out_ref[...] = total[...].astype(out_ref.dtype)

    cand_copy.wait_send()
    for copy in sent:
        copy.wait_send()


CHUNKS1 = 2


def body(queries, prefix_kv, cand_kv, lengths, out_weight):
    tokens, width = queries.shape
    hd = prefix_kv.shape[2]
    heads = width // hd
    positions = prefix_kv.shape[1]
    any_ = pl.BlockSpec(memory_space=pl.ANY)
    dma = pltpu.SemaphoreType.DMA
    return pl.pallas_call(
        attend_kernel,
        out_shape=jax.ShapeDtypeStruct((tokens, out_weight.shape[1]), BF),
        in_specs=[pl.BlockSpec(memory_space=pltpu.SMEM), any_, any_, any_, any_],
        out_specs=pl.BlockSpec(memory_space=pltpu.VMEM),
        scratch_shapes=[
            pltpu.VMEM((2, 8, positions, hd), BF),
            pltpu.VMEM((2, tokens, hd), BF),
            pltpu.VMEM((tokens, width), BF),
            pltpu.VMEM((heads, tokens, 2 * hd), BF),
            pltpu.VMEM(out_weight.shape, BF),
            pltpu.VMEM((heads, tokens, 2 * hd), F32),
            pltpu.VMEM((heads, tokens, hd), F32),
            pltpu.VMEM((8, 2, heads, tokens, hd), BF),
            pltpu.VMEM((tokens, out_weight.shape[1]), F32),
            dma((4,)),
            dma((2,)),
            dma((KINDS, CHUNKS1)),
            dma((8, CHUNKS1)),
            dma((8, CHUNKS1)),
            dma((KINDS, heads)),
            dma((8, heads)),
            dma((8, heads)),
        ],
        compiler_params=pltpu.CompilerParams(
            collective_id=0, has_side_effects=True, vmem_limit_bytes=60 * 1024 * 1024
        ),
        name="attend",
    )(lengths, queries, prefix_kv, cand_kv, out_weight)


def solution(mesh):
    placed = (
        P("ctx", "head"),
        P("head", "ctx", None),
        P("head", "ctx", None),
        P("ctx"),
        P(None, "head"),
    )
    return jax.shard_map(
        body, mesh=mesh, in_specs=placed, out_specs=P("ctx", "head"), check_vma=False
    )
```

time: 217 us -> 79.7 us (0.37)
  waiting for transfers between devices: 109 us -> 0 us
  Pallas kernels: 0 us -> 77.7 us
  matrix products: 64.1 us -> 0 us
  other arithmetic: 23.3 us -> 0 us
  between operations: 13.2 us -> 0.01 us
  local copies, waits for them, and re-layouts: 5.11 us -> 1.87 us
    all_gather x3 -> x0, waiting for transfers between devices: 108 us -> none  [the longest x1 51 us: body(): lax.all_gather(attended, 'head', axis=1, tiled=True)]
    pallas_call x0 -> x1, Pallas kernels: none -> 77.7 us  [body(): pl.pallas_call(attend_kernel, out_shape=jax.ShapeDtypeStruct((tokens, out...]
    dot_general x5 -> x0, matrix products: 64.1 us -> none  [the longest x1 26.2 us: absorb(): jnp.einsum('hrp,pd->hrd', probs.astype(jnp.bfloat16), value_block, prefer...]
    reduce_sum x2 -> x0, other arithmetic: 22.4 us -> none  [the longest x1 22.1 us: absorb(): row_total = row_total * shrink + jnp.sum(probs, axis=2)]
  transfers between devices with their start and end apart: 4 -> 0, of which waited for: 4 -> 0; matrix products, arithmetic and copies ran while one was open for 24% -> 0% of each run, Pallas kernels for 0% -> 0%
where the time goes in v1:
time: 79.7 us; the launch traced here: 79.6 us
  Pallas kernels  77.7 us (97%)
  local copies, waits for them, and re-layouts  1.87 us (2%)
    pallas_call x1, Pallas kernels, body(): pl.pallas_call(attend_kernel, out_shape=jax.ShapeDtypeStruct((tokens, out...  77.7 us
    unnamed x1, local copies, waits for them, and re-layouts  1.87 us

profile of v1, /device:TPU:1, one launch (start us, length us, event | category | flops | bytes accessed | tf_op | source)
XLA Modules:
  0.0 79.6 jit_solution(8839951677823919839)
XLA Ops:
  0.0 77.7 %attend.1 = bf16[512,512]{1,0:T(8,128)(2,1)} custom-call(s32[8]{0:T(128)} %lengths_ref.1, bf16[512,512]{1,0:T(8,128)(2,1)} %q_hbm.1, bf16[1,1024,128]{2,1,0:T(8,128)(2,1)} %pre_hbm.1, bf16[1,512,128]{2,1,0:T(8,128)(2,1)} %cand_hbm.1, bf16[8192,512]{1,0:T(8,128)(2,1)} %w_hbm.1), custom_call_target="tpu_custom_call" | custom-call | tf_op jit(solution)/shard_map/attend/pallas_call | solution.py:368
  77.7 1.9 %copy.7 = bf16[512,512]{1,0:T(8,128)(2,1)} copy(bf16[512,512]{1,0:T(8,128)(2,1)} %attend.1) | data formatting | bytes 1048576

commit v2 on v1

--- a/solution.py
+++ b/solution.py
@@ -14,8 +14,9 @@
 NEG_FILL = -1e30
 NT = (((1,), (1,)), ((), ()))
 
-FORWARD, BACK, ACROSS, OVER = 0, 1, 2, 3
+FORWARD, BACK, OVER = 0, 1, 2
 KINDS = 15
+CHUNKS1 = 2
 
 
 def attend_kernel(
@@ -36,8 +37,8 @@
     over1 = (y * 2 + 1 - x_hi, head)
     over2 = (ctx, z * 4 + (1 - x_lo) * 2 + core)
     sibling = (ctx, z * 4 + x_lo * 2 + 1 - core)
-    near1 = {FORWARD: ring1(1), BACK: ring1(3), ACROSS: ring1(2), OVER: over1}
-    near2 = {FORWARD: ring2(1), BACK: ring2(3), ACROSS: ring2(2), OVER: over2}
+    near1 = {FORWARD: ring1(1), BACK: ring1(3), OVER: over1}
+    near2 = {FORWARD: ring2(1), BACK: ring2(3), OVER: over2}
 
     barrier = pltpu.get_barrier_semaphore()
     others = [*near1.values(), *near2.values(), sibling]
@@ -82,7 +83,7 @@
         src = piece(slot, c)
         if phase == 1 and slot == 0:
             src = pre_hbm.at[0, pl.ds(c * rows1, rows1)]
-        copy = remote(src, piece(slot, c), ss.at[7 + slot, c], bb.at[slot, c], sibling)
+        copy = remote(src, piece(slot, c), ss.at[6 + slot, c], bb.at[slot, c], sibling)
         copy.start()
         sent.append(copy)
 
@@ -101,42 +102,40 @@
     def near(phase):
         return near1 if phase == 1 else near2
 
-    def own_near(phase, c):
+    def own(phase, c):
         n = near(phase)
-        send(phase, 0, 1, c, 3, n[OVER])
-        send(phase, 0, 3, c, 0, n[FORWARD])
-        send(phase, 0, 2, c, 1, n[BACK])
-
-    def own_far(phase, c):
-        send(phase, 0, 4, c, 2, near(phase)[ACROSS])
+        send(phase, 0, 1, c, 0, n[OVER])
+        send(phase, 0, 3, c, 1, n[FORWARD])
+        send(phase, 0, 2, c, 2, n[BACK])
+        share(phase, 0, c)
+
+    def on_near(phase, c):
+        arrived(phase, 2 + c % 2, c)
+        send(phase, 2 + c % 2, 4, c, 3, near(phase)[FORWARD if c % 2 else BACK])
+        share(phase, 2 + c % 2, c)
+        on_plain(phase, 3 - c % 2, c)
 
     def on_partner(phase, c):
         arrived(phase, 1, c)
-        n = near(phase)
-        send(phase, 1, 6, c, 4, n[FORWARD])
-        send(phase, 1, 5, c, 5, n[BACK])
+        send(phase, 1, 6, c, 4, near(phase)[FORWARD])
+        send(phase, 1, 5, c, 5, near(phase)[BACK])
         share(phase, 1, c)
 
     def on_far(phase, c):
         arrived(phase, 4, c)
-        send(phase, 4, 7, c, 6, near(phase)[OVER])
+        send(phase, 4, 7, c, 14, near(phase)[OVER])
         share(phase, 4, c)
+
+    def on_late(phase, c):
+        on_plain(phase, 5, c)
+        on_plain(phase, 6, c)
+
+    def on_last(phase, c):
+        on_plain(phase, 7, c)
 
     def on_plain(phase, slot, c):
         arrived(phase, slot, c)
         share(phase, slot, c)
-
-    pl.semaphore_wait(barrier, len(others))
-
-    cand_copy = remote(cand_hbm.at[0], cand.at[core], cand_sem.at[0], cand_sem.at[1], sibling)
-    cand_copy.start()
-    for c in range(CHUNKS1):
-        own_near(1, c)
-    for c in range(CHUNKS1):
-        share(1, 0, c)
-    for c in range(CHUNKS1):
-        own_far(1, c)
-    local[3].start()
 
     heads = q_two.shape[0]
     hd = kv.shape[3]
@@ -147,6 +146,14 @@
         high = scaled.astype(BF)
         q_two[h, :, :hd] = high
         q_two[h, :, hd:] = (scaled - high.astype(F32)).astype(BF)
+
+    pl.semaphore_wait(barrier, len(others))
+
+    cand_copy = remote(cand_hbm.at[0], cand.at[core], cand_sem.at[0], cand_sem.at[1], sibling)
+    cand_copy.start()
+    for c in range(CHUNKS1):
+        own(1, c)
+    local[3].start()
 
     tokens = q_two.shape[1]
     half = tokens // 2
@@ -207,58 +214,57 @@
             acc[h, r : r + half] = result
             row_max[h, r : r + half] = new
 
-    def block(slot, chosen):
+    def keys_of(kind, pieces):
+        parts = [kv[kind, slot, c * rows1 : (c + 1) * rows1] for slot, c in pieces]
+        return jnp.concatenate(parts, axis=0) if len(parts) > 1 else parts[0]
+
+    def attend(units):
         ahead(
-            chosen,
-            lambda h, r: scores(h, r, kv[0, slot]),
-            lambda s, h, r: absorb(s, h, r, kv[1, slot], False),
+            units,
+            lambda h, r, pieces, last: scores(h, r, keys_of(0, pieces)),
+            lambda s, h, r, pieces, last: absorb(s, h, r, keys_of(1, pieces), last),
         )
 
-    def both(slot):
-        return kv[0, slot], kv[1, slot]
+    def over(hs, pieces, last=False):
+        return [(h, r, pieces, last) for h in hs for r in (0, half)]
+
+    def whole(*chosen):
+        return [(slot, c) for slot in chosen for c in every1]
+
+    def await_shared(pieces):
+        for slot, c in pieces:
+            shared(1, slot, c)
 
     every1 = range(CHUNKS1)
     local[0].wait()
-    for c in every1:
-        shared(1, 0, c)
-    block(0, pairs)
-    for c in every1:
-        on_partner(1, c)
-    for slot in (2, 3):
-        for c in every1:
-            on_plain(1, slot, c)
-    for c in every1:
-        shared(1, 1, c)
-    block(1, pairs)
-    for c in every1:
-        on_far(1, c)
-    for c in every1:
-        shared(1, 2, c)
-    block(2, pairs)
-    for slot in (5, 6):
-        for c in every1:
-            on_plain(1, slot, c)
-    for c in every1:
-        shared(1, 3, c)
-    block(3, pairs)
-    for c in every1:
-        on_plain(1, 7, c)
-    for slot in (4, 5, 6, 7):
-        for c in every1:
-            shared(1, slot, c)
+    await_shared(whole(0))
+    attend(over((0, 1), whole(0)))
+    on_near(1, 0)
+    on_partner(1, 0)
+    attend(over((2, 3), whole(0)))
+    first, second = [(1, 0), (2, 0), (3, 0)], [(1, 1), (2, 1), (3, 1)]
+    await_shared(first)
+    attend(over((0, 1), first))
+    on_near(1, 1)
+    on_partner(1, 1)
+    attend(over((2, 3), first))
+    on_far(1, 0)
+    await_shared(second)
+    attend(over((0, 1), second))
+    on_far(1, 1)
+    on_late(1, 0)
+    attend(over((2, 3), second))
+    on_late(1, 1)
+    await_shared(whole(4))
+    attend(over(range(heads), whole(4)))
+    on_last(1, 0)
+    on_last(1, 1)
+    await_shared(whole(5, 6))
+    attend(over((0,), whole(5, 6)))
+    await_shared(whole(7))
 
     def finish(h):
-        units = [(h, r, j) for j in (0, 1) for r in (0, half)]
-
-        def first(h, r, j):
-            k = jnp.concatenate([kv[0, 4 + 2 * j], kv[0, 5 + 2 * j]], axis=0)
-            return scores(h, r, k)
-
-        def second(s, h, r, j):
-            v = jnp.concatenate([kv[1, 4 + 2 * j], kv[1, 5 + 2 * j]], axis=0)
-            absorb(s, h, r, v, j == 1)
-
-        ahead(units, first, second)
+        attend((over((h,), whole(5, 6)) if h else []) + over((h,), whole(7), True))
 
     wide = total.shape[1]
 
@@ -277,85 +283,64 @@
         )
         total[...] = product if first else total[...] + product
 
-    def launch(c):
-        own_near(2, c)
-        share(2, 0, c)
-        own_far(2, c)
-
-    finish(0)
-    launch(0)
-    finish(1)
-    launch(1)
-    finish(2)
-    launch(2)
-    on_partner(2, 0)
-    finish(3)
-    launch(3)
-
-    def near_slots(c):
-        on_plain(2, 2, c)
-        on_plain(2, 3, c)
-
-    def late_slots(c):
-        on_plain(2, 5, c)
-        on_plain(2, 6, c)
-
     def ready(slot, pair):
         shared(2, slot, 2 * pair)
         shared(2, slot, 2 * pair + 1)
 
-    near_slots(0)
+    def take(slot, pair):
+        ready(slot, pair)
+        project(slot, pair, slot == 0 and pair == 0)
+
+    finish(0)
+    own(2, 0)
+    finish(1)
+    own(2, 1)
+    finish(2)
+    own(2, 2)
+    on_near(2, 0)
+    finish(3)
+    own(2, 3)
+    on_near(2, 1)
+    on_partner(2, 0)
+    local[3].wait()
+    take(0, 0)
+    on_near(2, 2)
     on_partner(2, 1)
     on_far(2, 0)
-    local[3].wait()
-    ready(0, 0)
-    project(0, 0, True)
-    near_slots(1)
-    late_slots(0)
+    take(1, 0)
+    take(2, 0)
+    take(3, 0)
+    on_near(2, 3)
     on_partner(2, 2)
     on_far(2, 1)
-    on_plain(2, 7, 0)
-    ready(1, 0)
-    project(1, 0)
-    near_slots(2)
+    take(0, 1)
+    on_late(2, 0)
     on_partner(2, 3)
-    late_slots(1)
-    ready(2, 0)
-    project(2, 0)
-    ready(3, 0)
-    project(3, 0)
+    on_last(2, 0)
+    take(1, 1)
+    take(2, 1)
+    take(3, 1)
     on_far(2, 2)
-    ready(4, 0)
-    project(4, 0)
-    on_plain(2, 7, 1)
-    near_slots(3)
-    ready(5, 0)
-    project(5, 0)
-    late_slots(2)
-    ready(6, 0)
-    project(6, 0)
+    take(4, 0)
+    on_late(2, 1)
+    take(5, 0)
+    take(6, 0)
+    on_last(2, 1)
+    take(7, 0)
     on_far(2, 3)
-    ready(7, 0)
-    project(7, 0)
-    on_plain(2, 7, 2)
-    for slot in (0, 1, 2, 3):
-        ready(slot, 1)
-        project(slot, 1)
-    late_slots(3)
-    ready(4, 1)
-    project(4, 1)
-    on_plain(2, 7, 3)
-    for slot in (5, 6, 7):
-        ready(slot, 1)
-        project(slot, 1)
+    take(4, 1)
+    on_late(2, 2)
+    on_last(2, 2)
+    on_late(2, 3)
+    take(5, 1)
+    take(6, 1)
+    on_last(2, 3)
+    take(7, 1)
     out_ref[...] = total[...].astype(out_ref.dtype)
 
     cand_copy.wait_send()
     for copy in sent:
         copy.wait_send()
-
-
-CHUNKS1 = 2
 
 
 def body(queries, prefix_kv, cand_kv, lengths, out_weight):
@@ -364,6 +349,10 @@
     heads = width // hd
     positions = prefix_kv.shape[1]
     any_ = pl.BlockSpec(memory_space=pl.ANY)
+    args = [
+        pltpu.with_memory_space_constraint(a, pltpu.HBM)
+        for a in (lengths, queries, prefix_kv, cand_kv, out_weight)
+    ]
     dma = pltpu.SemaphoreType.DMA
     return pl.pallas_call(
         attend_kernel,
@@ -390,10 +379,10 @@
             dma((8, heads)),
         ],
         compiler_params=pltpu.CompilerParams(
-            collective_id=0, has_side_effects=True, vmem_limit_bytes=60 * 1024 * 1024
+            collective_id=0, has_side_effects=True, vmem_limit_bytes=48 * 1024 * 1024
         ),
         name="attend",
-    )(lengths, queries, prefix_kv, cand_kv, out_weight)
+    )(*args)
 
 
 def solution(mesh):

time: 79.7 us -> 68 us (0.85)
  Pallas kernels: 77.7 us -> 67 us
  local copies, waits for them, and re-layouts: 1.87 us -> 0.8 us
    pallas_call x1, Pallas kernels: 77.7 us -> 67 us  [body(): pl.pallas_call(attend_kernel, out_shape=jax.ShapeDtypeStruct((tokens, out...]
    unnamed x1, local copies, waits for them, and re-layouts: 1.87 us -> 0.8 us
where the time goes in v2:
time: 68 us; the launch traced here: 67.8 us
  Pallas kernels  67 us (99%)
  local copies, waits for them, and re-layouts  0.8 us (1%)
    pallas_call x1, Pallas kernels, body(): pl.pallas_call(attend_kernel, out_shape=jax.ShapeDtypeStruct((tokens, out...  67 us

profile of v2, /device:TPU:1, one launch (start us, length us, event | category | flops | bytes accessed | tf_op | source)
XLA Modules:
  0.0 67.8 jit_solution(4408736941914469454)
XLA Ops:
  0.0 67.0 %attend.1 = bf16[512,512]{1,0:T(8,128)(2,1)S(1)} custom-call(s32[8]{0:T(128)} %lengths_ref.1, bf16[512,512]{1,0:T(8,128)(2,1)} %q_hbm.1, bf16[1,1024,128]{2,1,0:T(8,128)(2,1)} %pre_hbm.1, bf16[1,512,128]{2,1,0:T(8,128)(2,1)} %cand_hbm.1, bf16[8192,512]{1,0:T(8,128)(2,1)} %w_hbm.1), custom_call_target="tpu_custom_call" | custom-call | tf_op jit(solution)/shard_map/attend/pallas_call | solution.py:357
  67.0 0.8 %copy.7 = bf16[512,512]{1,0:T(8,128)(2,1)} copy(bf16[512,512]{1,0:T(8,128)(2,1)S(1)} %attend.1) | data formatting | bytes 1048576

commit v3 on v2

--- a/solution.py
+++ b/solution.py
@@ -15,14 +15,91 @@
 NT = (((1,), (1,)), ((), ()))
 
 FORWARD, BACK, OVER = 0, 1, 2
-KINDS = 15
+KINDS = 17
 CHUNKS1 = 2
+ARRIVE, ATTEND, LAUNCH, PROJECT = range(4)
+SPLIT = 3
+SCHEDULE = (
+    (ATTEND, (3, ((0, 0), (0, 1))), (1, ((0, 1),)), (2, ((0, 0), (0, 1))), (0, ((0, 1),))),
+    (ARRIVE, 1, 2, 0),
+    (ARRIVE, 1, 3, 0),
+    (ATTEND, (0, ((0, 0),))),
+    (ARRIVE, 1, 2, 1),
+    (ARRIVE, 1, 3, 1),
+    (ARRIVE, 1, 1, 0),
+    (ARRIVE, 1, 1, 1),
+    (ATTEND, (2, ((2, 0), (3, 0))), (3, ((2, 0),)), (1, ((2, 0),)), (0, ((2, 0),))),
+    (ARRIVE, 1, 4, 0),
+    (ATTEND, (3, ((1, 0), (1, 1), (3, 1))), (1, ((0, 0), (1, 0))), (2, ((1, 0), (1, 1), (2, 1)))),
+    (ARRIVE, 1, 4, 1),
+    (ARRIVE, 1, 5, 0),
+    (ATTEND, (3, ((2, 1), (4, 0))), (1, ((1, 1), (3, 0), (3, 1), (4, 0))), (2, ((3, 1), (4, 0))), (0, ((3, 1),))),
+    (ARRIVE, 1, 6, 0),
+    (ARRIVE, 1, 5, 1),
+    (ATTEND, (2, ((4, 1), (5, 0))), (3, ((3, 0), (4, 1), (5, 0)))),
+    (ARRIVE, 1, 6, 1),
+    (ARRIVE, 1, 7, 0),
+    (ARRIVE, 1, 7, 1),
+    (ATTEND, (3, ((5, 1), (6, 0))), (2, ((5, 1), (6, 0))), (1, ((2, 1),))),
+    (ATTEND, (3, ((6, 1), (7, 0), (7, 1)))),
+    (LAUNCH, 3),
+    (ATTEND, (2, ((6, 1), (7, 0), (7, 1)))),
+    (LAUNCH, 2),
+    (ATTEND, (1, ((4, 1), (5, 0), (5, 1), (6, 0), (6, 1), (7, 0), (7, 1)))),
+    (LAUNCH, 1),
+    (ATTEND, (0, ((1, 0), (1, 1), (2, 1), (3, 0), (4, 0), (4, 1), (5, 0), (5, 1), (6, 0), (6, 1), (7, 0), (7, 1)))),
+    (ARRIVE, 2, 3, 3),
+    (LAUNCH, 0),
+    (ARRIVE, 2, 2, 2),
+    (ARRIVE, 2, 3, 2),
+    (ARRIVE, 2, 2, 3),
+    (ARRIVE, 2, 3, 1),
+    (ARRIVE, 2, 1, 3),
+    (ARRIVE, 2, 2, 0),
+    (ARRIVE, 2, 4, 3),
+    (ARRIVE, 2, 1, 2),
+    (ARRIVE, 2, 4, 2),
+    (ARRIVE, 2, 2, 1),
+    (ARRIVE, 2, 3, 0),
+    (ARRIVE, 2, 1, 0),
+    (PROJECT, 0, 1),
+    (ARRIVE, 2, 4, 1),
+    (ARRIVE, 2, 4, 0),
+    (ARRIVE, 2, 1, 1),
+    (ARRIVE, 2, 7, 2),
+    (ARRIVE, 2, 5, 2),
+    (PROJECT, 3, 1),
+    (PROJECT, 4, 1),
+    (ARRIVE, 2, 7, 3),
+    (PROJECT, 3, 0),
+    (PROJECT, 2, 1),
+    (ARRIVE, 2, 5, 3),
+    (PROJECT, 1, 1),
+    (ARRIVE, 2, 6, 3),
+    (PROJECT, 2, 0),
+    (PROJECT, 1, 0),
+    (ARRIVE, 2, 7, 1),
+    (PROJECT, 4, 0),
+    (ARRIVE, 2, 6, 2),
+    (PROJECT, 0, 0),
+    (ARRIVE, 2, 7, 0),
+    (ARRIVE, 2, 6, 0),
+    (PROJECT, 5, 1),
+    (ARRIVE, 2, 6, 1),
+    (ARRIVE, 2, 5, 0),
+    (ARRIVE, 2, 5, 1),
+    (PROJECT, 6, 1),
+    (PROJECT, 7, 1),
+    (PROJECT, 7, 0),
+    (PROJECT, 6, 0),
+    (PROJECT, 5, 0),
+)
 
 
 def attend_kernel(
-    lengths_ref, q_hbm, pre_hbm, cand_hbm, w_hbm, out_ref,
+    lengths_hbm, q_hbm, pre_hbm, cand_hbm, w_hbm, out_ref,
     kv, cand, q_raw, q_two, weights, acc, row_max, att, total,
-    local_sem, cand_sem, s1, r1, b1, s2, r2, b2,
+    lengths_ref, local_sem, cand_sem, s1, r1, b1, s2, r2, b2,
 ):
     ctx, head = lax.axis_index("ctx"), lax.axis_index("head")
     y, x_hi = ctx // 2, ctx % 2
@@ -50,8 +127,9 @@
         pltpu.make_async_copy(cand_hbm.at[0], cand.at[core], local_sem.at[1]),
         pltpu.make_async_copy(q_hbm, q_raw, local_sem.at[2]),
         pltpu.make_async_copy(w_hbm, weights, local_sem.at[3]),
+        pltpu.make_async_copy(lengths_hbm, lengths_ref, local_sem.at[4]),
     ]
-    for copy in local[:3]:
+    for copy in local[:3] + local[4:]:
         copy.start()
 
     def remote(src, dst, send, recv, device):
@@ -78,6 +156,15 @@
         copy.start()
         sent.append(copy)
 
+    def send_half(src_slot, dst_slot, part, kind, device):
+        rows = att.shape[3] // 2
+        src = piece2(src_slot, SPLIT).at[pl.ds(part * rows, rows)]
+        dst = piece2(dst_slot, SPLIT).at[pl.ds(part * rows, rows)]
+        recv = r2.at[dst_slot, SPLIT] if part == 0 else r2.at[dst_slot + 3, SPLIT]
+        copy = remote(src, dst, s2.at[kind, SPLIT], recv, device)
+        copy.start()
+        sent.append(copy)
+
     def share(phase, slot, c):
         piece, ss, bb = (piece1, s1, b1) if phase == 1 else (piece2, s2, b2)
         src = piece(slot, c)
@@ -90,7 +177,14 @@
     def arrived(phase, slot, c):
         piece, rr = (piece1, r1) if phase == 1 else (piece2, r2)
         ref = piece(slot, c)
-        remote(ref, ref, rr.at[slot, c], rr.at[slot, c], sibling).wait_recv()
+        if phase == 2 and c == SPLIT and slot in (5, 6):
+            for part in (0, 1):
+                rows = att.shape[3] // 2
+                half_ref = ref.at[pl.ds(part * rows, rows)]
+                sem = rr.at[slot + 3 * part, c]
+                remote(half_ref, half_ref, sem, sem, sibling).wait_recv()
+        else:
+            remote(ref, ref, rr.at[slot, c], rr.at[slot, c], sibling).wait_recv()
 
     def shared(phase, slot, c):
         if phase == 1:
@@ -109,32 +203,24 @@
         send(phase, 0, 2, c, 2, n[BACK])
         share(phase, 0, c)
 
-    def on_near(phase, c):
-        arrived(phase, 2 + c % 2, c)
-        send(phase, 2 + c % 2, 4, c, 3, near(phase)[FORWARD if c % 2 else BACK])
-        share(phase, 2 + c % 2, c)
-        on_plain(phase, 3 - c % 2, c)
-
-    def on_partner(phase, c):
-        arrived(phase, 1, c)
-        send(phase, 1, 6, c, 4, near(phase)[FORWARD])
-        send(phase, 1, 5, c, 5, near(phase)[BACK])
-        share(phase, 1, c)
-
-    def on_far(phase, c):
-        arrived(phase, 4, c)
-        send(phase, 4, 7, c, 14, near(phase)[OVER])
-        share(phase, 4, c)
-
-    def on_late(phase, c):
-        on_plain(phase, 5, c)
-        on_plain(phase, 6, c)
-
-    def on_last(phase, c):
-        on_plain(phase, 7, c)
-
-    def on_plain(phase, slot, c):
+    def on_arrival(phase, slot, c):
+        n = near(phase)
         arrived(phase, slot, c)
+        divided = phase == 2 and c == SPLIT
+        if slot == 1 and divided:
+            send_half(1, 6, 0, 4, n[FORWARD])
+            send_half(1, 5, 0, 5, n[BACK])
+        elif slot == 1:
+            send(phase, 1, 6, c, 4, n[FORWARD])
+            send(phase, 1, 5, c, 5, n[BACK])
+        if slot in (2, 3) and divided:
+            send_half(slot, slot + 3, 1, 13 + slot, n[OVER])
+        if slot == 2 and c % 2 == 0:
+            send(phase, 2, 4, c, 3, n[BACK])
+        if slot == 3 and c % 2 == 1:
+            send(phase, 3, 4, c, 3, n[FORWARD])
+        if slot == 4:
+            send(phase, 4, 7, c, 14, n[OVER])
         share(phase, slot, c)
 
     heads = q_two.shape[0]
@@ -176,6 +262,7 @@
             held = following
 
     local[1].wait()
+    local[4].wait()
     remote(cand.at[1 - core], cand.at[1 - core], cand_sem.at[0], cand_sem.at[1], sibling).wait_recv()
     slots = tokens // lengths_ref.shape[0]
     per = half // slots
@@ -224,47 +311,6 @@
             lambda h, r, pieces, last: scores(h, r, keys_of(0, pieces)),
             lambda s, h, r, pieces, last: absorb(s, h, r, keys_of(1, pieces), last),
         )
-
-    def over(hs, pieces, last=False):
-        return [(h, r, pieces, last) for h in hs for r in (0, half)]
-
-    def whole(*chosen):
-        return [(slot, c) for slot in chosen for c in every1]
-
-    def await_shared(pieces):
-        for slot, c in pieces:
-            shared(1, slot, c)
-
-    every1 = range(CHUNKS1)
-    local[0].wait()
-    await_shared(whole(0))
-    attend(over((0, 1), whole(0)))
-    on_near(1, 0)
-    on_partner(1, 0)
-    attend(over((2, 3), whole(0)))
-    first, second = [(1, 0), (2, 0), (3, 0)], [(1, 1), (2, 1), (3, 1)]
-    await_shared(first)
-    attend(over((0, 1), first))
-    on_near(1, 1)
-    on_partner(1, 1)
-    attend(over((2, 3), first))
-    on_far(1, 0)
-    await_shared(second)
-    attend(over((0, 1), second))
-    on_far(1, 1)
-    on_late(1, 0)
-    attend(over((2, 3), second))
-    on_late(1, 1)
-    await_shared(whole(4))
-    attend(over(range(heads), whole(4)))
-    on_last(1, 0)
-    on_last(1, 1)
-    await_shared(whole(5, 6))
-    attend(over((0,), whole(5, 6)))
-    await_shared(whole(7))
-
-    def finish(h):
-        attend((over((h,), whole(5, 6)) if h else []) + over((h,), whole(7), True))
 
     wide = total.shape[1]
 
@@ -283,59 +329,31 @@
         )
         total[...] = product if first else total[...] + product
 
-    def ready(slot, pair):
-        shared(2, slot, 2 * pair)
-        shared(2, slot, 2 * pair + 1)
-
-    def take(slot, pair):
-        ready(slot, pair)
-        project(slot, pair, slot == 0 and pair == 0)
-
-    finish(0)
-    own(2, 0)
-    finish(1)
-    own(2, 1)
-    finish(2)
-    own(2, 2)
-    on_near(2, 0)
-    finish(3)
-    own(2, 3)
-    on_near(2, 1)
-    on_partner(2, 0)
-    local[3].wait()
-    take(0, 0)
-    on_near(2, 2)
-    on_partner(2, 1)
-    on_far(2, 0)
-    take(1, 0)
-    take(2, 0)
-    take(3, 0)
-    on_near(2, 3)
-    on_partner(2, 2)
-    on_far(2, 1)
-    take(0, 1)
-    on_late(2, 0)
-    on_partner(2, 3)
-    on_last(2, 0)
-    take(1, 1)
-    take(2, 1)
-    take(3, 1)
-    on_far(2, 2)
-    take(4, 0)
-    on_late(2, 1)
-    take(5, 0)
-    take(6, 0)
-    on_last(2, 1)
-    take(7, 0)
-    on_far(2, 3)
-    take(4, 1)
-    on_late(2, 2)
-    on_last(2, 2)
-    on_late(2, 3)
-    take(5, 1)
-    take(6, 1)
-    on_last(2, 3)
-    take(7, 1)
+    local[0].wait()
+    here, left, projected = set(), [8 * CHUNKS1] * heads, 0
+    for step in SCHEDULE:
+        if step[0] == ARRIVE:
+            on_arrival(*step[1:])
+        elif step[0] == ATTEND:
+            units = []
+            for h, pieces in step[1:]:
+                for piece in pieces:
+                    if piece not in here:
+                        here.add(piece)
+                        shared(1, *piece)
+                left[h] -= len(pieces)
+                units += [(h, r, pieces, left[h] == 0) for r in (0, half)]
+            attend(units)
+        elif step[0] == LAUNCH:
+            own(2, step[1])
+        else:
+            slot, pair = step[1:]
+            shared(2, slot, 2 * pair)
+            shared(2, slot, 2 * pair + 1)
+            if projected == 0:
+                local[3].wait()
+            project(slot, pair, projected == 0)
+            projected += 1
     out_ref[...] = total[...].astype(out_ref.dtype)
 
     cand_copy.wait_send()
@@ -357,7 +375,7 @@
     return pl.pallas_call(
         attend_kernel,
         out_shape=jax.ShapeDtypeStruct((tokens, out_weight.shape[1]), BF),
-        in_specs=[pl.BlockSpec(memory_space=pltpu.SMEM), any_, any_, any_, any_],
+        in_specs=[any_] * 5,
         out_specs=pl.BlockSpec(memory_space=pltpu.VMEM),
         scratch_shapes=[
             pltpu.VMEM((2, 8, positions, hd), BF),
@@ -369,13 +387,14 @@
             pltpu.VMEM((heads, tokens, hd), F32),
             pltpu.VMEM((8, 2, heads, tokens, hd), BF),
             pltpu.VMEM((tokens, out_weight.shape[1]), F32),
-            dma((4,)),
+            pltpu.SMEM(lengths.shape, jnp.int32),
+            dma((5,)),
             dma((2,)),
             dma((KINDS, CHUNKS1)),
             dma((8, CHUNKS1)),
             dma((8, CHUNKS1)),
             dma((KINDS, heads)),
-            dma((8, heads)),
+            dma((10, heads)),
             dma((8, heads)),
         ],
         compiler_params=pltpu.CompilerParams(

time: 68 us -> 64.1 us (0.943)
  Pallas kernels: 67 us -> 63.2 us
    pallas_call x1, Pallas kernels: 67 us -> 63.2 us  [body(): pl.pallas_call(attend_kernel, out_shape=jax.ShapeDtypeStruct((tokens, out...]
where the time goes in v3:
time: 64.1 us; the launch traced here: 64 us
  Pallas kernels  63.2 us (99%)
  local copies, waits for them, and re-layouts  0.8 us (1%)
    pallas_call x1, Pallas kernels, body(): pl.pallas_call(attend_kernel, out_shape=jax.ShapeDtypeStruct((tokens, out...  63.2 us

profile of v3, /device:TPU:1, one launch (start us, length us, event | category | flops | bytes accessed | tf_op | source)
XLA Modules:
  0.0 64.0 jit_solution(16304228936384662322)
XLA Ops:
  0.0 63.2 %attend.1 = bf16[512,512]{1,0:T(8,128)(2,1)S(1)} custom-call(s32[8]{0:T(128)} %lengths_hbm.1, bf16[512,512]{1,0:T(8,128)(2,1)} %q_hbm.1, bf16[1,1024,128]{2,1,0:T(8,128)(2,1)} %pre_hbm.1, bf16[1,512,128]{2,1,0:T(8,128)(2,1)} %cand_hbm.1, bf16[8192,512]{1,0:T(8,128)(2,1)} %w_hbm.1), custom_call_target="tpu_custom_call" | custom-call | tf_op jit(solution)/shard_map/attend/pallas_call | solution.py:375
  63.2 0.8 %copy.7 = bf16[512,512]{1,0:T(8,128)(2,1)} copy(bf16[512,512]{1,0:T(8,128)(2,1)S(1)} %attend.1) | data formatting | bytes 1048576

commit v4 on v3

--- a/solution.py
+++ b/solution.py
@@ -15,84 +15,83 @@
 NT = (((1,), (1,)), ((), ()))
 
 FORWARD, BACK, OVER = 0, 1, 2
-KINDS = 17
+KINDS = 15
 CHUNKS1 = 2
 ARRIVE, ATTEND, LAUNCH, PROJECT = range(4)
-SPLIT = 3
+TURNED = 2
 SCHEDULE = (
-    (ATTEND, (3, ((0, 0), (0, 1))), (1, ((0, 1),)), (2, ((0, 0), (0, 1))), (0, ((0, 1),))),
     (ARRIVE, 1, 2, 0),
+    (ATTEND, (0, ((0, 1),)), (1, ((0, 0), (0, 1))), (2, ((0, 0),))),
     (ARRIVE, 1, 3, 0),
-    (ATTEND, (0, ((0, 0),))),
     (ARRIVE, 1, 2, 1),
     (ARRIVE, 1, 3, 1),
     (ARRIVE, 1, 1, 0),
     (ARRIVE, 1, 1, 1),
-    (ATTEND, (2, ((2, 0), (3, 0))), (3, ((2, 0),)), (1, ((2, 0),)), (0, ((2, 0),))),
+    (ATTEND, (3, ((0, 1), (3, 0))), (2, ((2, 0), (3, 0))), (0, ((0, 0),))),
     (ARRIVE, 1, 4, 0),
-    (ATTEND, (3, ((1, 0), (1, 1), (3, 1))), (1, ((0, 0), (1, 0))), (2, ((1, 0), (1, 1), (2, 1)))),
+    (ATTEND, (0, ((1, 0), (1, 1), (2, 0), (2, 1))), (3, ((0, 0), (2, 0), (2, 1))), (2, ((2, 1),))),
     (ARRIVE, 1, 4, 1),
     (ARRIVE, 1, 5, 0),
-    (ATTEND, (3, ((2, 1), (4, 0))), (1, ((1, 1), (3, 0), (3, 1), (4, 0))), (2, ((3, 1), (4, 0))), (0, ((3, 1),))),
+    (ATTEND, (3, ((1, 0), (1, 1), (4, 0))), (0, ((3, 0), (3, 1), (4, 0))), (2, ((4, 0),)), (1, ((1, 0),))),
     (ARRIVE, 1, 6, 0),
     (ARRIVE, 1, 5, 1),
-    (ATTEND, (2, ((4, 1), (5, 0))), (3, ((3, 0), (4, 1), (5, 0)))),
+    (ATTEND, (3, ((3, 1), (5, 0))), (2, ((0, 1), (3, 1), (5, 0))), (0, ((5, 0),))),
     (ARRIVE, 1, 6, 1),
     (ARRIVE, 1, 7, 0),
     (ARRIVE, 1, 7, 1),
-    (ATTEND, (3, ((5, 1), (6, 0))), (2, ((5, 1), (6, 0))), (1, ((2, 1),))),
+    (ATTEND, (3, ((4, 1), (5, 1), (6, 0))), (0, ((4, 1), (6, 0))), (2, ((1, 1),))),
     (ATTEND, (3, ((6, 1), (7, 0), (7, 1)))),
     (LAUNCH, 3),
-    (ATTEND, (2, ((6, 1), (7, 0), (7, 1)))),
+    (ATTEND, (0, ((5, 1), (6, 1), (7, 0), (7, 1)))),
+    (LAUNCH, 0),
+    (ATTEND, (2, ((1, 0), (4, 1), (5, 1), (6, 0), (6, 1), (7, 0), (7, 1)))),
     (LAUNCH, 2),
-    (ATTEND, (1, ((4, 1), (5, 0), (5, 1), (6, 0), (6, 1), (7, 0), (7, 1)))),
+    (ATTEND, (1, ((1, 1), (2, 0), (2, 1), (3, 0), (3, 1), (4, 0), (4, 1), (5, 0), (5, 1), (6, 0), (6, 1), (7, 0), (7, 1)))),
     (LAUNCH, 1),
-    (ATTEND, (0, ((1, 0), (1, 1), (2, 1), (3, 0), (4, 0), (4, 1), (5, 0), (5, 1), (6, 0), (6, 1), (7, 0), (7, 1)))),
+    (ARRIVE, 2, 2, 0),
+    (ARRIVE, 2, 3, 2),
+    (ARRIVE, 2, 2, 2),
     (ARRIVE, 2, 3, 3),
-    (LAUNCH, 0),
-    (ARRIVE, 2, 2, 2),
-    (ARRIVE, 2, 3, 2),
+    (ARRIVE, 2, 3, 1),
+    (PROJECT, 3, 1),
+    (ARRIVE, 2, 1, 3),
+    (ARRIVE, 2, 1, 2),
+    (ARRIVE, 2, 3, 0),
+    (ARRIVE, 2, 4, 3),
+    (ARRIVE, 2, 1, 0),
+    (ARRIVE, 2, 1, 1),
+    (PROJECT, 0, 1),
+    (ARRIVE, 2, 4, 2),
+    (ARRIVE, 2, 4, 0),
+    (ARRIVE, 2, 4, 1),
+    (ARRIVE, 2, 7, 3),
+    (ARRIVE, 2, 2, 1),
+    (ARRIVE, 2, 5, 2),
+    (ARRIVE, 2, 6, 3),
     (ARRIVE, 2, 2, 3),
-    (ARRIVE, 2, 3, 1),
-    (ARRIVE, 2, 1, 3),
-    (ARRIVE, 2, 2, 0),
-    (ARRIVE, 2, 4, 3),
-    (ARRIVE, 2, 1, 2),
-    (ARRIVE, 2, 4, 2),
-    (ARRIVE, 2, 2, 1),
-    (ARRIVE, 2, 3, 0),
-    (ARRIVE, 2, 1, 0),
-    (PROJECT, 0, 1),
-    (ARRIVE, 2, 4, 1),
-    (ARRIVE, 2, 4, 0),
-    (ARRIVE, 2, 1, 1),
+    (PROJECT, 1, 0),
+    (PROJECT, 0, 0),
+    (PROJECT, 4, 0),
+    (PROJECT, 4, 1),
+    (ARRIVE, 2, 6, 2),
+    (PROJECT, 2, 0),
+    (ARRIVE, 2, 6, 0),
+    (PROJECT, 3, 0),
+    (ARRIVE, 2, 5, 0),
+    (ARRIVE, 2, 5, 3),
+    (PROJECT, 6, 1),
+    (PROJECT, 2, 1),
+    (ARRIVE, 2, 6, 1),
+    (PROJECT, 1, 1),
+    (ARRIVE, 2, 5, 1),
+    (ARRIVE, 2, 7, 0),
+    (ARRIVE, 2, 7, 1),
+    (PROJECT, 5, 1),
     (ARRIVE, 2, 7, 2),
-    (ARRIVE, 2, 5, 2),
-    (PROJECT, 3, 1),
-    (PROJECT, 4, 1),
-    (ARRIVE, 2, 7, 3),
-    (PROJECT, 3, 0),
-    (PROJECT, 2, 1),
-    (ARRIVE, 2, 5, 3),
-    (PROJECT, 1, 1),
-    (ARRIVE, 2, 6, 3),
-    (PROJECT, 2, 0),
-    (PROJECT, 1, 0),
-    (ARRIVE, 2, 7, 1),
-    (PROJECT, 4, 0),
-    (ARRIVE, 2, 6, 2),
-    (PROJECT, 0, 0),
-    (ARRIVE, 2, 7, 0),
-    (ARRIVE, 2, 6, 0),
-    (PROJECT, 5, 1),
-    (ARRIVE, 2, 6, 1),
-    (ARRIVE, 2, 5, 0),
-    (ARRIVE, 2, 5, 1),
-    (PROJECT, 6, 1),
-    (PROJECT, 7, 1),
-    (PROJECT, 7, 0),
     (PROJECT, 6, 0),
     (PROJECT, 5, 0),
+    (PROJECT, 7, 0),
+    (PROJECT, 7, 1),
 )
 
 
@@ -156,15 +155,6 @@
         copy.start()
         sent.append(copy)
 
-    def send_half(src_slot, dst_slot, part, kind, device):
-        rows = att.shape[3] // 2
-        src = piece2(src_slot, SPLIT).at[pl.ds(part * rows, rows)]
-        dst = piece2(dst_slot, SPLIT).at[pl.ds(part * rows, rows)]
-        recv = r2.at[dst_slot, SPLIT] if part == 0 else r2.at[dst_slot + 3, SPLIT]
-        copy = remote(src, dst, s2.at[kind, SPLIT], recv, device)
-        copy.start()
-        sent.append(copy)
-
     def share(phase, slot, c):
         piece, ss, bb = (piece1, s1, b1) if phase == 1 else (piece2, s2, b2)
         src = piece(slot, c)
@@ -177,14 +167,7 @@
     def arrived(phase, slot, c):
         piece, rr = (piece1, r1) if phase == 1 else (piece2, r2)
         ref = piece(slot, c)
-        if phase == 2 and c == SPLIT and slot in (5, 6):
-            for part in (0, 1):
-                rows = att.shape[3] // 2
-                half_ref = ref.at[pl.ds(part * rows, rows)]
-                sem = rr.at[slot + 3 * part, c]
-                remote(half_ref, half_ref, sem, sem, sibling).wait_recv()
-        else:
-            remote(ref, ref, rr.at[slot, c], rr.at[slot, c], sibling).wait_recv()
+        remote(ref, ref, rr.at[slot, c], rr.at[slot, c], sibling).wait_recv()
 
     def shared(phase, slot, c):
         if phase == 1:
@@ -206,20 +189,19 @@
     def on_arrival(phase, slot, c):
         n = near(phase)
         arrived(phase, slot, c)
-        divided = phase == 2 and c == SPLIT
-        if slot == 1 and divided:
-            send_half(1, 6, 0, 4, n[FORWARD])
-            send_half(1, 5, 0, 5, n[BACK])
-        elif slot == 1:
+        turned = phase == 2 and c == TURNED
+        if slot == 1 and not turned:
             send(phase, 1, 6, c, 4, n[FORWARD])
             send(phase, 1, 5, c, 5, n[BACK])
-        if slot in (2, 3) and divided:
-            send_half(slot, slot + 3, 1, 13 + slot, n[OVER])
+        if slot in (2, 3) and turned:
+            send(phase, slot, slot + 3, c, 2 + slot, n[OVER])
+        if slot == 5 + c % 2 and turned:
+            send(phase, slot, 7, c, 14, n[FORWARD if c % 2 else BACK])
         if slot == 2 and c % 2 == 0:
             send(phase, 2, 4, c, 3, n[BACK])
         if slot == 3 and c % 2 == 1:
             send(phase, 3, 4, c, 3, n[FORWARD])
-        if slot == 4:
+        if slot == 4 and not turned:
             send(phase, 4, 7, c, 14, n[OVER])
         share(phase, slot, c)
 
@@ -394,7 +376,7 @@
             dma((8, CHUNKS1)),
             dma((8, CHUNKS1)),
             dma((KINDS, heads)),
-            dma((10, heads)),
+            dma((8, heads)),
             dma((8, heads)),
         ],
         compiler_params=pltpu.CompilerParams(

time: 64.1 us -> 63.5 us (level)
  no operation moved by 1% of the time
where the time goes in v4:
time: 63.5 us; the launch traced here: 63.4 us
  Pallas kernels  62.6 us (99%)
  local copies, waits for them, and re-layouts  0.8 us (1%)
    pallas_call x1, Pallas kernels, body(): pl.pallas_call(attend_kernel, out_shape=jax.ShapeDtypeStruct((tokens, out...  62.6 us

profile of v4, /device:TPU:1, one launch (start us, length us, event | category | flops | bytes accessed | tf_op | source)
XLA Modules:
  0.0 63.4 jit_solution(5630021745254453041)
XLA Ops:
  0.0 62.6 %attend.1 = bf16[512,512]{1,0:T(8,128)(2,1)S(1)} custom-call(s32[8]{0:T(128)} %lengths_hbm.1, bf16[512,512]{1,0:T(8,128)(2,1)} %q_hbm.1, bf16[1,1024,128]{2,1,0:T(8,128)(2,1)} %pre_hbm.1, bf16[1,512,128]{2,1,0:T(8,128)(2,1)} %cand_hbm.1, bf16[8192,512]{1,0:T(8,128)(2,1)} %w_hbm.1), custom_call_target="tpu_custom_call" | custom-call | tf_op jit(solution)/shard_map/attend/pallas_call | solution.py:357
  62.6 0.8 %copy.7 = bf16[512,512]{1,0:T(8,128)(2,1)} copy(bf16[512,512]{1,0:T(8,128)(2,1)S(1)} %attend.1) | data formatting | bytes 1048576

commit v5 on v4

--- a/solution.py
+++ b/solution.py
@@ -35,12 +35,12 @@
     (ATTEND, (3, ((1, 0), (1, 1), (4, 0))), (0, ((3, 0), (3, 1), (4, 0))), (2, ((4, 0),)), (1, ((1, 0),))),
     (ARRIVE, 1, 6, 0),
     (ARRIVE, 1, 5, 1),
+    (ARRIVE, 1, 7, 0),
     (ATTEND, (3, ((3, 1), (5, 0))), (2, ((0, 1), (3, 1), (5, 0))), (0, ((5, 0),))),
     (ARRIVE, 1, 6, 1),
-    (ARRIVE, 1, 7, 0),
     (ARRIVE, 1, 7, 1),
-    (ATTEND, (3, ((4, 1), (5, 1), (6, 0))), (0, ((4, 1), (6, 0))), (2, ((1, 1),))),
-    (ATTEND, (3, ((6, 1), (7, 0), (7, 1)))),
+    (ATTEND, (3, ((4, 1), (5, 1), (6, 0), (7, 0))), (0, ((4, 1), (6, 0))), (2, ((1, 1),))),
+    (ATTEND, (3, ((6, 1), (7, 1)))),
     (LAUNCH, 3),
     (ATTEND, (0, ((5, 1), (6, 1), (7, 0), (7, 1)))),
     (LAUNCH, 0),
@@ -87,9 +87,9 @@
     (ARRIVE, 2, 7, 0),
     (ARRIVE, 2, 7, 1),
     (PROJECT, 5, 1),
-    (ARRIVE, 2, 7, 2),
     (PROJECT, 6, 0),
     (PROJECT, 5, 0),
+    (ARRIVE, 2, 7, 2),
     (PROJECT, 7, 0),
     (PROJECT, 7, 1),
 )

time: 63.5 us -> 63.6 us (level)
  no operation moved by 1% of the time
where the time goes in v5:
time: 63.6 us; the launch traced here: 63.5 us
  Pallas kernels  62.7 us (99%)
  local copies, waits for them, and re-layouts  0.8 us (1%)
    pallas_call x1, Pallas kernels, body(): pl.pallas_call(attend_kernel, out_shape=jax.ShapeDtypeStruct((tokens, out...  62.7 us

profile of v5, /device:TPU:1, one launch (start us, length us, event | category | flops | bytes accessed | tf_op | source)
XLA Modules:
  0.0 63.5 jit_solution(5201477341683160680)
XLA Ops:
  0.0 62.7 %attend.1 = bf16[512,512]{1,0:T(8,128)(2,1)S(1)} custom-call(s32[8]{0:T(128)} %lengths_hbm.1, bf16[512,512]{1,0:T(8,128)(2,1)} %q_hbm.1, bf16[1,1024,128]{2,1,0:T(8,128)(2,1)} %pre_hbm.1, bf16[1,512,128]{2,1,0:T(8,128)(2,1)} %cand_hbm.1, bf16[8192,512]{1,0:T(8,128)(2,1)} %w_hbm.1), custom_call_target="tpu_custom_call" | custom-call | tf_op jit(solution)/shard_map/attend/pallas_call | solution.py:357
  62.7 0.8 %copy.7 = bf16[512,512]{1,0:T(8,128)(2,1)} copy(bf16[512,512]{1,0:T(8,128)(2,1)S(1)} %attend.1) | data formatting | bytes 1048576
